TPU v7x, 512 devices: a whole 4x4x16 slice. The times are simulated.
512 devices in a mesh: node: 16 (over z), tp: 32 (over x, y, core).
Axes of the slice: x: 4, y: 4, z: 16, core: 2. Of those that a mesh axis runs over, the one named last changes fastest.
Arguments:
- suffix_hidden: bfloat16 [4096, 7168], P('node', 'tp'), may hold values from -6 to 6
- suffix_adapter: int32 [16], replicated, may hold values from 0 to 3
- page_owner: int32 [16, 16, 1], replicated, may hold values from 0 to 15; in each aligned block of 16 rows (0 to 15, 16 to 31, ..., all dimensions but the last counted through in order) at most 2 rows name the same one
- page_number: int32 [16, 16], replicated, may hold values from 0 to 63
- prefix_page_count: int32 [16], replicated, may hold values from 8 to 16, as said below
- suffix_node: int32 [16], replicated, may hold values from 0 to 15, each once
- prefix_cache: bfloat16 [1024, 64, 576], P('node', 'tp'), may hold values from -210 to 210
- query_down_weight: bfloat16 [7168, 1536], P('tp'), may hold values from -0.0625 to 0.0625
- kv_down_weight: bfloat16 [7168, 576], P('tp'), may hold values from -0.0625 to 0.0625
- adapter_down_panels: bfloat16 [4, 7168, 64], P(None, 'tp'), may hold values from -0.0625 to 0.0625
- adapter_query_up: bfloat16 [4, 32, 1536], replicated, may hold values from -1 to 1
- adapter_kv_up: bfloat16 [4, 32, 576], replicated, may hold values from -1 to 1
- latent_query_gain: float32 [1536], replicated, may hold values from 0.25 to 2
- latent_kv_gain: float32 [512], replicated, may hold values from 0.25 to 2
- query_up_weight: bfloat16 [1536, 12288], P(None, 'tp'), may hold values from -0.15625 to 0.15625
- key_up_weight: bfloat16 [64, 128, 512], P('tp'), may hold values from -0.25 to 0.25
- value_up_weight: bfloat16 [64, 512, 128], P('tp'), may hold values from -0.25 to 0.25
Outputs:
- values: bfloat16 [4096, 8192], P('node', 'tp')
Inputs may be any that keep to these rules, and one draw needn't show every extreme that they name: `page_owner`: among the 16 entries of one suffix's list no node is named more than 2 times, a bound that some block reaches. `prefix_page_count`: some suffix has exactly 16 pages. `suffix_node`: each node serves exactly one suffix.
All inputs are finite; a program needn't handle non-finite values.
Results may differ from a plain program's by a relative error of at most 0.035.
Values may be sent and summed in bfloat16 or wider, within the bound.
No kernel may reach another device: no remote copies, remote signals or barrier semaphores. Data moves between devices by JAX's collectives and lax.ppermute only.
A program may use at most 64 MiB of HBM per device.

v0:
```python
import math

import jax
import jax.numpy as jnp
from jax import lax
from jax.sharding import PartitionSpec as P

PAGE = 64
MAXP = 16


def rope_apply(vectors, token_positions):
    half = vectors.shape[1] // 2
    steps = jnp.arange(half, dtype=jnp.float32)
    freqs = jnp.power(jnp.float32(10000.0), -2.0 * steps / vectors.shape[1])
    angles = token_positions[:, None] * freqs[None, :]
    first = vectors[:, :half]
    second = vectors[:, half:]
    cosine = jnp.cos(angles)
    sine = jnp.sin(angles)
    return jnp.concatenate([first * cosine - second * sine, first * sine + second * cosine], axis=1)


def normalize(vectors, gain):
    mean_square = jnp.mean(vectors * vectors, axis=1, keepdims=True)
    return vectors * lax.rsqrt(mean_square + 1e-06) * gain[None, :]


def finalize(
    unnormed,
    adapter_choice,
    token_positions,
    adapter_query_up,
    adapter_kv_up,
    latent_query_gain,
    latent_kv_gain,
):
    latent_query_span = adapter_query_up.shape[2]
    latent_kv_span = adapter_kv_up.shape[2]
    adapter_rank = adapter_query_up.shape[1]
    latent = latent_kv_gain.shape[0]
    lowrank = unnormed[:, latent_query_span + latent_kv_span :].astype(jnp.bfloat16)
    query_panel = lax.dynamic_index_in_dim(adapter_query_up, adapter_choice, 0, keepdims=False)
    kv_panel = lax.dynamic_index_in_dim(adapter_kv_up, adapter_choice, 0, keepdims=False)
    q_raw = unnormed[:, :latent_query_span] + jnp.dot(
        lowrank[:, :adapter_rank], query_panel, preferred_element_type=jnp.float32
    )
    kv_raw = unnormed[:, latent_query_span : latent_query_span + latent_kv_span] + jnp.dot(
        lowrank[:, adapter_rank:], kv_panel, preferred_element_type=jnp.float32
    )
    query_latent = normalize(q_raw, latent_query_gain).astype(jnp.bfloat16)
    compressed = normalize(kv_raw[:, :latent], latent_kv_gain)
    rotated = rope_apply(kv_raw[:, latent:], token_positions)
    local_keys = jnp.concatenate([compressed, rotated], axis=1).astype(jnp.bfloat16)
    return (query_latent, local_keys)


def attend(query, prefix_keys, prefix_valid, local_keys, scale, latent):
    contract = (((1,), (1,)), ((), ()))
    far = lax.dot_general(query, prefix_keys, contract, preferred_element_type=jnp.float32) * scale
    near = lax.dot_general(query, local_keys, contract, preferred_element_type=jnp.float32) * scale
    far = jnp.where(prefix_valid[None, :], far, -jnp.inf)
    count = query.shape[0]
    places = jnp.arange(count, dtype=jnp.int32)
    near = jnp.where(places[:, None] >= places[None, :], near, -jnp.inf)
    top = jnp.maximum(jnp.max(far, axis=1), jnp.max(near, axis=1))
    far_exp = jnp.exp(far - top[:, None])
    near_exp = jnp.exp(near - top[:, None])
    total = jnp.sum(far_exp, axis=1) + jnp.sum(near_exp, axis=1)
    mixed = jnp.dot(
        far_exp.astype(jnp.bfloat16), prefix_keys[:, :latent], preferred_element_type=jnp.float32
    )
    mixed = mixed + jnp.dot(
        near_exp.astype(jnp.bfloat16), local_keys[:, :latent], preferred_element_type=jnp.float32
    )
    return (mixed / total[:, None]).astype(jnp.bfloat16)


def head_output(
    q_head, token_positions, key_up, value_up, prefix_keys, prefix_valid, local_keys, scale
):
    nope = key_up.shape[0]
    q_rope = rope_apply(q_head[:, nope:].astype(jnp.float32), token_positions).astype(jnp.bfloat16)
    q_abs = jnp.dot(q_head[:, :nope], key_up, preferred_element_type=jnp.float32).astype(
        jnp.bfloat16
    )
    query = jnp.concatenate([q_abs, q_rope], axis=1)
    latent_out = attend(query, prefix_keys, prefix_valid, local_keys, scale, key_up.shape[1])
    return jnp.dot(latent_out, value_up, preferred_element_type=jnp.float32).astype(jnp.bfloat16)


def on_device(
    suffix_hidden,
    suffix_adapter,
    page_owner,
    page_number,
    prefix_page_count,
    suffix_node,
    prefix_cache,
    query_down_weight,
    kv_down_weight,
    adapter_down_panels,
    adapter_query_up,
    adapter_kv_up,
    latent_query_gain,
    latent_kv_gain,
    query_up_weight,
    key_up_weight,
    value_up_weight,
):
    nodes = lax.axis_size("node")
    myself = lax.axis_index("node")
    capacity = 2 * MAXP // nodes
    order = jnp.arange(nodes, dtype=jnp.int32)
    suffix_at = jnp.sum(
        jnp.where(suffix_node[None, :] == order[:, None], order[None, :], 0), axis=1
    )
    mine = lax.dynamic_index_in_dim(suffix_at, myself, 0, keepdims=False)
    adapter_choice = lax.dynamic_index_in_dim(suffix_adapter, mine, 0, keepdims=False)
    length = lax.dynamic_index_in_dim(prefix_page_count, mine, 0, keepdims=False)
    adapter_local = lax.dynamic_index_in_dim(adapter_down_panels, adapter_choice, 0, keepdims=False)
    token_count = suffix_hidden.shape[0]
    key_width = prefix_cache.shape[2]
    token_positions = (length * PAGE + jnp.arange(token_count, dtype=jnp.int32)).astype(jnp.float32)
    unnormed = lax.psum(
        jnp.concatenate(
            [
                jnp.dot(suffix_hidden, query_down_weight, preferred_element_type=jnp.float32),
                jnp.dot(suffix_hidden, kv_down_weight, preferred_element_type=jnp.float32),
                jnp.dot(suffix_hidden, adapter_local, preferred_element_type=jnp.float32),
            ],
            axis=1,
        ),
        "tp",
    )
    query_latent, local_keys = finalize(
        unnormed,
        adapter_choice,
        token_positions,
        adapter_query_up,
        adapter_kv_up,
        latent_query_gain,
        latent_kv_gain,
    )
    holders_all = jnp.take(page_owner[:, :, 0], suffix_at, axis=0)
    index_all = jnp.take(page_number, suffix_at, axis=0)
    is_mine = holders_all == myself
    sender_rank = jnp.cumsum(is_mine.astype(jnp.int32), axis=1) - 1
    slot_order = jnp.arange(capacity, dtype=jnp.int32)
    picked = is_mine[:, None, :] & (sender_rank[:, None, :] == slot_order[None, :, None])
    page_ids = jnp.sum(jnp.where(picked, index_all[:, None, :], 0), axis=2)
    outgoing = jnp.take(prefix_cache, page_ids, axis=0)
    incoming = lax.all_to_all(outgoing, "node", split_axis=0, concat_axis=0, tiled=True)
    received = incoming.reshape(nodes * capacity, incoming.shape[2], key_width)
    my_holders = lax.dynamic_index_in_dim(page_owner[:, :, 0], mine, 0, keepdims=False)
    entries = jnp.arange(MAXP, dtype=jnp.int32)
    live = entries < length
    per_holder = jnp.sum(
        ((my_holders[None, :] == order[:, None]) & live[None, :]).astype(jnp.int32), axis=1
    )
    slot_valid = (slot_order[None, :] < per_holder[:, None]).reshape(nodes * capacity)
    keys = lax.all_gather(received, "tp", axis=1, tiled=True)
    prefix_valid = jnp.repeat(slot_valid, PAGE)
    prefix_keys = keys.reshape(keys.shape[0] * keys.shape[1], key_width)
    q_all = jnp.dot(query_latent, query_up_weight, preferred_element_type=jnp.float32).astype(
        jnp.bfloat16
    )
    heads_local = key_up_weight.shape[0]
    head_width = query_up_weight.shape[1] // heads_local
    scale = 1.0 / math.sqrt(head_width)
    outputs = []
    for head in range(heads_local):
        q_head = q_all[:, head * head_width : (head + 1) * head_width]
        outputs.append(
            head_output(
                q_head,
                token_positions,
                key_up_weight[head],
                value_up_weight[head],
                prefix_keys,
                prefix_valid,
                local_keys,
                scale,
            )
        )
    return jnp.concatenate(outputs, axis=1)


def solution(mesh):
    return jax.shard_map(
        on_device,
        mesh=mesh,
        in_specs=(
            P("node", "tp"),
            P(),
            P(),
            P(),
            P(),
            P(),
            P("node", "tp", None),
            P("tp", None),
            P("tp", None),
            P(None, "tp", None),
            P(),
            P(),
            P(),
            P(),
            P(None, "tp"),
            P("tp", None, None),
            P("tp", None, None),
        ),
        out_specs=P("node", "tp"),
        check_vma=False,
    )
```

profile of v0, /device:TPU:1, one launch (start us, length us, event | category | flops | bytes accessed | tf_op | source)
XLA Modules:
  0.0 249.3 jit_solution(12365762770283247503)
XLA Ops:
  6.5 0.9 select_reduce_fusion.1
  7.4 0.6 dynamic_slice.26
  10.0 1.2 dynamic_slice.29
  12.5 1.3 fusion.122
  13.8 1.6 fusion.121
  16.1 0.9 convolution_bitcast_fusion
  17.0 1.6 pad_maximum_fusion
  18.6 0.0 all-reduce.2.cloned.1.call-update
  18.6 0.0 all-gather.2.cloned.1.call-start
  18.7 0.6 copy-done.7
  19.3 0.6 gather_fusion.2
  19.8 0.6 gather_fusion.1
  20.4 0.1 fusion.116
  20.5 0.2 reduce_window_sum.11
  20.6 0.1 broadcast_select_fusion.1
  20.7 0.1 select_reduce_fusion
  20.8 0.1 copy.78
  20.9 0.1 reshape.119
  21.0 0.1 copy.77
  21.1 0.7 gather_fusion
  21.9 0.2 broadcast_select_fusion
  22.0 0.1 copy.79
  22.1 27.3 %all_to_all.5 = bf16[16,2,2,576]{3,1,2,0:T(2,128)(2,1)S(1)} all-to-all(bf16[16,2,2,576]{3,1,2,0:T(2,128)(2,1)S(1)} %copy.79), channel_id=1, replica_groups=mesh['node'=16,'tp'=32] {'node'}, dimensions={0} | all-to-all | bytes 147456 | tf_op jit(solution)/shard_map/all_to_all | solution.py:153
  49.4 0.1 copy.80
  49.5 0.6 copy.81
  50.2 0.0 all-gather.2.cloned.1.call-update
  50.2 0.6 dynamic_slice.28
  51.5 0.6 iota_compare_fusion.5
  52.1 0.1 convert_reduce_fusion
  52.2 0.1 iota_compare_fusion.4
  52.3 0.1 lt.76
  52.4 0.1 broadcast_in_dim.70
  52.5 0.1 broadcast_in_dim.104
  52.6 109.5 %all-reduce.2.cloned.1.call-done = f32[256,2176]{0,1:T(8,128)} async-done(((f32[256,2176]{0,1:T(8,128)}), f32[256,2176]{0,1:T(8,128)}) %all-reduce.2.cloned.1.call-update) | async-done | bytes 2228240 | tf_op jit(solution)/shard_map/psum | solution.py:125
  162.1 1.9 convert.22
  164.0 0.4 copy-done.1
  164.4 1.4 multiply_reduce_fusion
  165.8 0.9 convolution_convert_fusion.2
  166.8 1.1 convolution_add_fusion.1
  167.8 0.2 fusion.91
  168.1 0.1 copy.84
  168.2 0.1 copy.83
  168.3 0.1 copy.76
  168.4 0.1 copy.75
  168.5 0.1 multiply_reduce_fusion.1
  168.6 0.2 convolution_convert_fusion
  168.9 0.1 multiply_convert_fusion.2
  169.0 0.4 fusion.118
  169.4 0.2 convolution_convert_fusion.1
  169.7 0.4 fusion.120
  170.0 55.8 %all-gather.2.cloned.1.call-done = bf16[32,64,576]{2,0,1:T(8,128)(2,1)} async-done(((bf16[32,2,576]{2,0,1:T(8,128)(2,1)}), bf16[32,64,576]{2,0,1:T(8,128)(2,1)}) %all-gather.2.cloned.1.call-update) | async-done | bytes 2359312 | tf_op jit(solution)/shard_map/all_gather | solution.py:162
  225.9 2.6 %copy.82 = bf16[32,64,576]{2,1,0:T(8,128)(2,1)S(1)} copy(bf16[32,64,576]{2,0,1:T(8,128)(2,1)} %all-gather.2.cloned.1.call-done) | data formatting | bytes 4718592 | tf_op jit(solution)/shard_map/all_gather | solution.py:162
  228.5 1.2 fusion.117
  229.7 1.3 fusion.58
  231.0 0.1 fusion.56
  231.1 1.2 fusion.119
  232.2 1.3 fusion.60
  233.6 0.1 fusion.54
  233.7 0.4 fusion.4
  234.1 0.4 fusion.2
  234.6 1.1 copy-done.4
  235.7 2.7 %fusion.39 = bf16[256,128]{0,1:T(8,128)(2,1)S(1)} fusion(f32[256,512]{1,0:T(8,128)} %fusion.58, bf16[2048,576]{1,0:T(8,128)(2,1)} %bitcast.50, f32[256,2048]{1,0:T(8,128)S(1)} %copy-done.4, f32[256]{0:T(256)S(1)} %max.15, f32[256]{0:T(256)S(1)} %add.129, bf16[2,512,128]{2,1,0:T(8,128)(2,1)} %param.35), kind=kOutput, calls=%fused_computation.38 | convolution fusion | flops 571899904 | bytes 4917248 | tf_op jit(solution)/shard_map/dot_general | solution.py:89
  238.4 3.3 %fusion.36 = bf16[256,128]{0,1:T(8,128)(2,1)S(1)} fusion(f32[256,512]{1,0:T(8,128)} %fusion.60, bf16[2048,576]{1,0:T(8,128)(2,1)} %bitcast.51, f32[256,2048]{1,0:T(8,128)} %copy-done.5, f32[256]{0:T(256)S(1)} %max.14, f32[256]{0:T(256)S(1)} %add.126, bf16[2,512,128]{2,1,0:T(8,128)(2,1)} %param.35), kind=kOutput, calls=%fused_computation.37 | convolution fusion | flops 571899904 | bytes 4917248 | tf_op jit(solution)/shard_map/dot_general | solution.py:89
  241.7 0.8 copy.85
  (43 shorter events, 0.2 us)
Async XLA Ops:
  6.5 159.3 %copy-start = (bf16[1536,384]{1,0:T(8,128)(2,1)S(1)}, bf16[1536,384]{1,0:T(8,128)(2,1)}, u32[]{:S(2)}) copy-start(bf16[1536,384]{1,0:T(8,128)(2,1)} %param.33) | copy-start | bytes 3538948
  6.5 9.5 %copy-start.6 = (bf16[256,224]{0,1:T(8,128)(2,1)S(1)}, bf16[256,224]{0,1:T(8,128)(2,1)}, u32[]{:S(2)}) copy-start(bf16[256,224]{0,1:T(8,128)(2,1)} %param.19) | copy-start | bytes 344068
  6.5 155.6 %all-reduce.2.cloned.1.call-start = ((), (), s32[]{:S(2)}) async-start(), calls=%async_computation.1 | async-start | bytes 4456448 | tf_op jit(solution)/shard_map/psum | solution.py:125
  18.6 0.7 copy-start.7
  18.6 1.3 copy-start.8
  18.6 2.6 %copy-start.10 = (bf16[64,2,576]{2,1,0:T(2,128)(2,1)S(1)}, bf16[64,2,576]{2,1,0:T(2,128)(2,1)}, u32[]{:S(2)}) copy-start(bf16[64,2,576]{2,1,0:T(2,128)(2,1)} %param.25) | copy-start | bytes 442372
  18.6 31.6 %copy-start.13 = (s32[16]{0:T(128)S(1)}, s32[16]{0:T(128)}, u32[]{:S(2)}) copy-start(s32[16]{0:T(128)} %param.23) | copy-start | bytes 196
  18.6 207.3 %all-gather.2.cloned.1.call-start = ((), (), s32[]{:S(2)}) async-start(), calls=%async_computation.2 | async-start | bytes 2703360 | tf_op jit(solution)/shard_map/all_gather | solution.py:162
  162.1 2.3 copy-start.1
  164.4 1.4 copy-start.11
  165.8 2.8 %copy-start.9 = (bf16[2,128,512]{2,1,0:T(8,128)(2,1)S(1)}, bf16[2,128,512]{2,1,0:T(8,128)(2,1)}, u32[]{:S(2)}) copy-start(bf16[2,128,512]{2,1,0:T(8,128)(2,1)} %param.34) | copy-start | bytes 786436
  166.7 2.2 copy-start.12
  228.5 2.6 %copy-start.2 = (bf16[32,64,576]{2,1,0:T(8,128)(2,1)}, bf16[32,64,576]{2,1,0:T(8,128)(2,1)S(1)}, u32[]{:S(2)}) copy-start(bf16[32,64,576]{2,1,0:T(8,128)(2,1)S(1)} %copy.82) | copy-start | bytes 7077892
  229.7 4.0 %copy-start.3 = (f32[256,2048]{1,0:T(8,128)}, f32[256,2048]{1,0:T(8,128)S(1)}, u32[]{:S(2)}) copy-start(f32[256,2048]{1,0:T(8,128)S(1)} %get-tuple-element.23) | copy-start | bytes 6291460
  232.2 2.3 copy-start.5
  234.1 1.6 copy-start.4
Sparse Core Ops, SparseCore 0:
  18.7 143.3 all-reduce.1
  165.7 60.1 all-gather.1
where the time goes:
time: 250 us; the launch traced here: 249 us
  waiting for transfers between devices  165 us (66%)
  blocking collectives  27.3 us (11%)
  matrix products  19.4 us (8%)
  between operations  18.3 us (7%)
  local copies, waits for them, and re-layouts  11.6 us (5%)
  other arithmetic  7.3 us (3%)
    psum x1, waiting for transfers between devices, on_device(): lax.psum(jnp.concatenate([jnp.dot(suffix_hidden, query_down_weight, prefe...  109 us
    all_gather x1, waiting for transfers between devices, on_device(): keys = lax.all_gather(received, 'tp', axis=1, tiled=True)  55.8 us
    all_to_all x1, blocking collectives, on_device(): lax.all_to_all(outgoing, 'node', split_axis=0, concat_axis=0, tiled=True)  27.3 us
    dot_general x2, matrix products, head_output(): jnp.dot(latent_out, value_up, preferred_element_type=jnp.float32)  6 us
  transfers between devices with their start and end apart: 2, of which 2 were waited for; matrix products, arithmetic and copies ran while one was open for 5% of the time, Pallas kernels for 0%

commit v1 on v0

v1 whole, which is shorter than its diff:
```python
import math

import jax
import jax.numpy as jnp
import numpy as np
from jax import lax
from jax.experimental import pallas as pl
from jax.experimental.pallas import tpu as pltpu
from jax.sharding import Mesh
from jax.sharding import PartitionSpec as P

F32 = jnp.float32
BF16 = jnp.bfloat16

PAGE = 64
MAXP = 16
SUFLEN = 256
NODES = 16
CHIPS = 16
HALF = SUFLEN // 2
ROWS = HALF // CHIPS
Q = 1536
LATENT = 512
ROPE = 64
KEY = LATENT + ROPE
RANK = 32
DOWN = Q + KEY + 2 * RANK
CHUNKS = 4
PAGEW = 640
GROUPS = 1 + CHUNKS
ROPES = Q + GROUPS * LATENT
BLOCK = ROPES + 3 * 128
SENDS = ((0, 1024), (1024, DOWN))
NOPE = 128
HEADW = NOPE + ROPE
VDIM = 128

FACTOR = math.log2(math.e) / math.sqrt(HEADW)
NT = (((1,), (1,)), ((), ()))
VMEM = pl.BlockSpec(memory_space=pltpu.VMEM)
HBM = pl.BlockSpec(memory_space=pltpu.HBM)
SMEM = pl.BlockSpec(memory_space=pltpu.SMEM)


def mm(a, b):
    return jnp.dot(a, b, preferred_element_type=F32)


def mmt(a, b):
    return lax.dot_general(a, b, NT, preferred_element_type=F32)


def iota(shape, dim):
    return lax.broadcasted_iota(jnp.int32, shape, dim)


def rope_tables():
    freqs = 10000.0 ** (-2.0 * np.arange(ROPE // 2) / ROPE)
    lanes = np.tile(freqs, 4)[None, :]
    base = np.arange(MAXP + 1)[:, None] * PAGE * lanes
    step = np.arange(SUFLEN)[:, None] * lanes
    return [t.astype(np.float32) for t in (np.cos(base), np.sin(base), np.cos(step), np.sin(step))]


def my_suffix(node_ref):
    me = lax.axis_index("node")
    mine = jnp.int32(0)
    for s in range(NODES):
        mine = jnp.where(node_ref[s] == me, s, mine)
    return me, mine


def down_kernel(
    node_hbm, adapter_hbm, x_hbm, wq_hbm, wkv_hbm, panels_hbm, keep_ref, *refs
):
    send_refs, (node_ref, adapter_ref, x_ref, wq_ref, wkv_ref, panels_ref, sems) = refs[: len(SENDS)], refs[len(SENDS) :]
    sources = (x_hbm, wq_hbm, wkv_hbm, panels_hbm, node_hbm, adapter_hbm)
    targets = (x_ref, wq_ref, wkv_ref, panels_ref, node_ref, adapter_ref)
    copies = [pltpu.make_async_copy(src, dst, sems.at[i]) for i, (src, dst) in enumerate(zip(sources, targets))]
    for copy in copies:
        copy.start()
    for copy in copies:
        copy.wait()
    _, mine = my_suffix(node_ref)
    core = lax.axis_index("core")
    x = x_ref[...].T
    cut = SENDS[0][1]
    tail = [mm(x, wq_ref[:, cut:]), mm(x, wkv_ref[...]), mmt(x, panels_ref[adapter_ref[mine]])]
    parts = [mm(x, wq_ref[:, :cut]), jnp.concatenate(tail, axis=1)]

    @pl.when(core == 0)
    def _():
        for (lo, hi), part, send_ref in zip(SENDS, parts, send_refs):
            keep_ref[:, lo:hi] = part[:HALF]
            send_ref[...] = part[HALF:]

    @pl.when(core != 0)
    def _():
        for (lo, hi), part, send_ref in zip(SENDS, parts, send_refs):
            keep_ref[:, lo:hi] = part[HALF:]
            send_ref[...] = part[:HALF]


def pages_kernel(node_hbm, owner_hbm, number_hbm, cache_hbm, pages_ref, node_row, owner_ref, number_ref, cache_ref, sems):
    copies = [
        pltpu.make_async_copy(source, target, sems.at[i])
        for i, (source, target) in enumerate(
            [(cache_hbm, cache_ref), (node_hbm, node_row), (owner_hbm, owner_ref), (number_hbm, number_ref)]
        )
    ]
    for copy in copies:
        copy.start()
    for copy in copies[1:]:
        copy.wait()
    me = lax.axis_index("node")
    count = NODES * 8
    node_of = iota((count, NODES), 0) // 8
    within = iota((count, 1), 0) % 8
    slot = within // 2
    expand = (node_row[...] == node_of).astype(BF16)
    owner = mm(expand, owner_ref[...].reshape(NODES, MAXP).astype(BF16))
    number = mm(expand, number_ref[...].astype(BF16))
    held = owner == me.astype(F32)
    before = (iota((MAXP, MAXP), 0) < iota((MAXP, MAXP), 1)).astype(BF16)
    rank = mm(held.astype(BF16), before)
    picked = held & (rank == slot.astype(F32))
    page = jnp.sum(jnp.where(picked, number + 1.0, 0.0), axis=1, keepdims=True).astype(jnp.int32) - 1
    row = 2 * page + within % 2
    select = (iota((count, 128), 1) == row) & (page >= 0)
    copies[0].wait()
    pages_ref[:, :KEY] = mm(select.astype(BF16), cache_ref[...].reshape(128, KEY)).astype(BF16)
    pages_ref[:, KEY:] = jnp.zeros((count, PAGEW - KEY), BF16)


def add_kernel(keep_ref, *refs):
    *swapped_refs, out_ref = refs
    for (lo, hi), swapped_ref in zip(SENDS, swapped_refs):
        out_ref[:, lo:hi] = (keep_ref[:, lo:hi] + swapped_ref[...]).astype(BF16)


def angles(length, rows, cb_ref, sb_ref, ct_ref, st_ref):
    cb = cb_ref[pl.ds(length, 1), :]
    sb = sb_ref[pl.ds(length, 1), :]
    ct = ct_ref[rows, :]
    st = st_ref[rows, :]
    return cb * ct - sb * st, sb * ct + cb * st


def turn(v):
    half = ROPE // 2
    parts = []
    for g in range(v.shape[1] // ROPE):
        parts.append(-v[:, g * ROPE + half : (g + 1) * ROPE])
        parts.append(v[:, g * ROPE : g * ROPE + half])
    return jnp.concatenate(parts, axis=1)


def finish_kernel(
    node_ref,
    adapter_ref,
    length_ref,
    node_row,
    owner_ref,
    parts_ref,
    pages_ref,
    aq_ref,
    akv_ref,
    gq_ref,
    gkv_ref,
    cb_ref,
    sb_ref,
    ct_ref,
    st_ref,
    out_ref,
):
    me, mine = my_suffix(node_ref)
    adapter = adapter_ref[mine]
    length = length_ref[mine]
    core = lax.axis_index("core")
    chip = lax.axis_index("x") * 4 + lax.axis_index("y")
    first = pl.multiple_of(core * HALF + chip * ROWS, ROWS)
    down = parts_ref[0].astype(F32)
    for i in range(1, CHIPS):
        down = down + parts_ref[i].astype(F32)
    low = down[:, Q + KEY :].astype(BF16)
    q_raw = down[:, :Q] + mm(low[:, :RANK], aq_ref[adapter])
    kv_raw = down[:, Q : Q + KEY] + mm(low[:, RANK:], akv_ref[adapter])
    q_lat = q_raw * lax.rsqrt(jnp.mean(q_raw * q_raw, axis=1, keepdims=True) + 1e-06) * gq_ref[...][None, :]
    c = kv_raw[:, :LATENT]
    c = c * lax.rsqrt(jnp.mean(c * c, axis=1, keepdims=True) + 1e-06) * gkv_ref[...][None, :]
    k = kv_raw[:, LATENT:]
    cosine, sine = angles(length, pl.ds(first, ROWS), cb_ref, sb_ref, ct_ref, st_ref)
    k = k * cosine[:, :ROPE] + turn(k) * sine[:, :ROPE]

    count = MAXP * 2
    pick = (node_row[...] == me).astype(BF16)
    mine_owner = mm(pick, owner_ref[...].reshape(NODES, MAXP).astype(BF16))
    entry = iota((count, MAXP), 0) // 2
    lane = iota((count, MAXP), 1)
    holder = jnp.sum(jnp.where(lane == entry, mine_owner, 0.0), axis=1, keepdims=True)
    earlier = (mine_owner == holder) & (lane < entry)
    rank = jnp.sum(earlier.astype(F32), axis=1, keepdims=True)
    source = holder.astype(jnp.int32) * 8 + rank.astype(jnp.int32) * 2 + iota((count, 1), 0) % 2
    select = (iota((count, 128), 1) == source).astype(BF16)
    prefix = mm(select, pages_ref[...])[:, :KEY]
    chunks = [prefix[g * ROWS : (g + 1) * ROWS] for g in range(CHUNKS)]
    pieces = [q_lat, c] + [p[:, :LATENT] for p in chunks]
    pieces += [k] + [p[:, LATENT:] for p in chunks] + [jnp.zeros((ROWS, ROPE), F32)]
    block = jnp.concatenate(pieces, axis=1).astype(BF16)
    for i in range(CHIPS):
        out_ref[i] = block


def attend_kernel(
    node_ref, length_ref, mine_ref, other_ref, wq_ref, wk_ref, wv_ref, cb_ref, sb_ref, ct_ref, st_ref, out_ref
):
    _, mine = my_suffix(node_ref)
    length = length_ref[mine]
    core = lax.axis_index("core")
    rows_a = pl.ds(pl.multiple_of(core * HALF, HALF), HALF)
    rows_b = pl.ds(pl.multiple_of((1 - core) * HALF, HALF), HALF)

    def both(lo, hi):
        return jnp.concatenate([mine_ref[:, lo:hi], other_ref[:, lo:hi]], axis=0)

    q_all = mm(both(0, Q), wq_ref[...]).astype(BF16)
    ca, sa = angles(length, rows_a, cb_ref, sb_ref, ct_ref, st_ref)
    cb, sb = angles(length, rows_b, cb_ref, sb_ref, ct_ref, st_ref)
    cosine = jnp.concatenate([ca, cb], axis=0)
    sine = jnp.concatenate([sa, sb], axis=0)
    ropes = jnp.concatenate([q_all[:, NOPE:HEADW], q_all[:, HEADW + NOPE :]], axis=1).astype(F32)
    ropes = (ropes * cosine + turn(ropes) * sine).astype(BF16)
    rope = jnp.concatenate([ropes[:, :ROPE], ropes[:, ROPE:]], axis=0)
    zero = jnp.zeros_like(rope)
    absorbed = [mm(q_all[:, h * HEADW : h * HEADW + NOPE], wk_ref[h]).astype(BF16) for h in range(2)]
    absorbed = jnp.concatenate(absorbed, axis=0)
    query = (jnp.concatenate([absorbed, rope, zero], axis=1), jnp.concatenate([absorbed, zero, rope], axis=1))
    latents = [both(Q + g * LATENT, Q + (g + 1) * LATENT) for g in range(GROUPS)]

    count = 2 * SUFLEN
    place = iota((count, SUFLEN), 0) % SUFLEN
    place = jnp.where(place < HALF, place + core * HALF, place - core * HALF)
    spot = iota((count, SUFLEN), 1)
    page = (spot % 8) // 2
    spot = jnp.where(spot < HALF, spot + core * HALF, spot - core * HALF)
    scores = []
    for g in range(GROUPS):
        tile = ROPES + g // 2 * 128
        s = mmt(query[g % 2], jnp.concatenate([latents[g], both(tile, tile + 128)], axis=1))
        if g == 0:
            s = jnp.where(place >= spot, s, -jnp.inf)
        elif g > 2:
            s = jnp.where(page + 4 * (g - 1) < length, s, -jnp.inf)
        scores.append(s)
    top = scores[0]
    for s in scores[1:]:
        top = jnp.maximum(top, s)
    top = jnp.max(top, axis=1, keepdims=True)
    weights = [jnp.exp2((s - top) * FACTOR) for s in scores]
    total = weights[0]
    for w in weights[1:]:
        total = total + w
    total = jnp.sum(total, axis=1, keepdims=True)
    mixed = jnp.zeros((count, LATENT), F32)
    for g in range(GROUPS):
        mixed = mixed + mm(weights[g].astype(BF16), latents[g])
    latent = (mixed / total).astype(BF16)
    for h in range(2):
        values = mm(latent[h * SUFLEN : (h + 1) * SUFLEN], wv_ref[h]).astype(BF16)
        out_ref[rows_a, h * VDIM : (h + 1) * VDIM] = values[:HALF]
        out_ref[rows_b, h * VDIM : (h + 1) * VDIM] = values[HALF:]


def on_device(
    suffix_hidden,
    suffix_adapter,
    page_owner,
    page_number,
    prefix_page_count,
    suffix_node,
    prefix_cache,
    query_down_weight,
    kv_down_weight,
    adapter_down_panels,
    adapter_query_up,
    adapter_kv_up,
    latent_query_gain,
    latent_kv_gain,
    query_up_weight,
    key_up_weight,
    value_up_weight,
):
    alone = pltpu.CompilerParams(vmem_limit_bytes=60 * 1024 * 1024)
    params = pltpu.CompilerParams(vmem_limit_bytes=40 * 1024 * 1024)
    tables = [jnp.asarray(t) for t in rope_tables()]
    owner = jnp.transpose(page_owner, (0, 2, 1))
    node_row = suffix_node.reshape(1, NODES)
    swap = [(0, 1), (1, 0)]

    outgoing = pl.pallas_call(
        pages_kernel,
        out_shape=jax.ShapeDtypeStruct((NODES * 8, PAGEW), BF16),
        in_specs=[HBM] * 4,
        out_specs=VMEM,
        scratch_shapes=[
            pltpu.VMEM((1, NODES), jnp.int32),
            pltpu.VMEM((NODES, 1, MAXP), jnp.int32),
            pltpu.VMEM((NODES, MAXP), jnp.int32),
            pltpu.VMEM(prefix_cache.shape, BF16),
            pltpu.SemaphoreType.DMA((4,)),
        ],
        compiler_params=alone,
        cost_estimate=pl.CostEstimate(flops=20_000_000, bytes_accessed=300_000, transcendentals=0),
        name="pages",
    )(node_row, owner, page_number, prefix_cache)
    received = lax.all_to_all(outgoing.reshape(NODES, 8, PAGEW), "node", 0, 0, tiled=True)
    hidden, _ = lax.optimization_barrier((suffix_hidden, outgoing))
    keep, *send = pl.pallas_call(
        down_kernel,
        out_shape=[jax.ShapeDtypeStruct((HALF, DOWN), F32)] + [jax.ShapeDtypeStruct((HALF, hi - lo), F32) for lo, hi in SENDS],
        in_specs=[HBM] * 6,
        out_specs=[VMEM] * (1 + len(SENDS)),
        scratch_shapes=[
            pltpu.SMEM((NODES,), jnp.int32),
            pltpu.SMEM((NODES,), jnp.int32),
            pltpu.VMEM((224, SUFLEN), BF16),
            pltpu.VMEM((224, Q), BF16),
            pltpu.VMEM((224, KEY), BF16),
            pltpu.VMEM((4, 2 * RANK, 224), BF16),
            pltpu.SemaphoreType.DMA((6,)),
        ],
        compiler_params=alone,
        cost_estimate=pl.CostEstimate(flops=1000, bytes_accessed=1000, transcendentals=0),
        name="down",
    )(
        suffix_node,
        suffix_adapter,
        hidden.T,
        query_down_weight,
        kv_down_weight,
        jnp.transpose(adapter_down_panels, (0, 2, 1)),
    )
    swapped = [lax.ppermute(part, "core", swap) for part in send]
    partial = pl.pallas_call(
        add_kernel,
        out_shape=jax.ShapeDtypeStruct((HALF, DOWN), BF16),
        in_specs=[VMEM] * (1 + len(SENDS)),
        out_specs=VMEM,
        compiler_params=params,
        cost_estimate=pl.CostEstimate(flops=1000, bytes_accessed=1000, transcendentals=0),
        name="add",
    )(keep, *swapped).reshape(CHIPS, ROWS, DOWN)
    parts = lax.all_to_all(partial, ("x", "y"), 0, 0, tiled=True)

    block = pl.pallas_call(
        finish_kernel,
        out_shape=jax.ShapeDtypeStruct((CHIPS, ROWS, BLOCK), BF16),
        in_specs=[SMEM] * 3 + [VMEM] * 12,
        out_specs=VMEM,
        compiler_params=params,
        name="finish",
    )(
        suffix_node,
        suffix_adapter,
        prefix_page_count,
        node_row,
        owner,
        parts,
        received.reshape(NODES * 8, PAGEW),
        adapter_query_up,
        adapter_kv_up,
        latent_query_gain,
        latent_kv_gain,
        *tables,
    )
    gathered = lax.all_to_all(block, ("x", "y"), 0, 0, tiled=True).reshape(HALF, BLOCK)
    other = lax.ppermute(gathered, "core", swap)
    return pl.pallas_call(
        attend_kernel,
        out_shape=jax.ShapeDtypeStruct((SUFLEN, 2 * VDIM), BF16),
        in_specs=[SMEM] * 2 + [VMEM] * 9,
        out_specs=VMEM,
        compiler_params=params,
        name="attend",
    )(
        suffix_node,
        prefix_page_count,
        gathered,
        other,
        query_up_weight,
        key_up_weight,
        value_up_weight,
        *tables,
    )


def solution(mesh):
    inner = Mesh(mesh.devices.reshape(NODES, 4, 4, 2), ("node", "x", "y", "core"))
    tp = ("x", "y", "core")
    return jax.shard_map(
        on_device,
        mesh=inner,
        in_specs=(
            P("node", tp),
            P(),
            P(),
            P(),
            P(),
            P(),
            P("node", tp, None),
            P(tp, None),
            P(tp, None),
            P(None, tp, None),
            P(),
            P(),
            P(),
            P(),
            P(None, tp),
            P(tp, None, None),
            P(tp, None, None),
        ),
        out_specs=P("node", tp),
        check_vma=False,
    )
```

time: 250 us -> 80.1 us (0.32)
  waiting for transfers between devices: 165 us -> 5.01 us
  starting transfers between devices: 0.04 us -> 29.6 us
  matrix products: 19.4 us -> 0 us
  between operations: 18.3 us -> 0.22 us
  Pallas kernels: 0 us -> 12.1 us
  local copies, waits for them, and re-layouts: 11.6 us -> 1.33 us
  other arithmetic: 7.3 us -> 0 us
  blocking collectives: 27.3 us -> 31 us
    psum x1 -> x0, waiting for transfers between devices: 109 us -> none  [on_device(): lax.psum(jnp.concatenate([jnp.dot(suffix_hidden, query_down_weight, prefe...]
    all_gather x1 -> x0, waiting for transfers between devices: 55.8 us -> none  [on_device(): keys = lax.all_gather(received, 'tp', axis=1, tiled=True)]
    dot_general x16 -> x0, matrix products: 19.4 us -> none  [the longest x2 6 us: head_output(): jnp.dot(latent_out, value_up, preferred_element_type=jnp.float32)]
    all_to_all x0 -> x1, starting transfers between devices: none -> 15.8 us  [on_device(): lax.all_to_all(outgoing.reshape(NODES, 8, PAGEW), 'node', 0, 0, tiled=True)]
    ppermute x0 -> x3, starting transfers between devices: none -> 13.8 us  [the longest x1 9.08 us: on_device(): other = lax.ppermute(gathered, 'core', swap)]
    pallas_call x0 -> x5, Pallas kernels: none -> 12.1 us  [the longest x1 5.46 us: on_device(): pl.pallas_call(attend_kernel, out_shape=jax.ShapeDtypeStruct((SUFLEN, 2 *...]
    ppermute x0 -> x3, waiting for transfers between devices: none -> 4.49 us  [the longest x1 2.41 us: on_device(): other = lax.ppermute(gathered, 'core', swap)]
    all_to_all x1 -> x2, blocking collectives: 27.3 us -> 31 us  [the longest x1 15.9 us: on_device(): parts = lax.all_to_all(partial, ('x', 'y'), 0, 0, tiled=True)]
  transfers between devices with their start and end apart: 2 -> 4, of which waited for: 2 -> 3; matrix products, arithmetic and copies ran while one was open for 5% -> 0% of each run, Pallas kernels for 0% -> 4%
where the time goes in v1:
time: 80.1 us; the launch traced here: 79.3 us
  blocking collectives  31 us (39%)
  starting transfers between devices  29.6 us (37%)
  Pallas kernels  12.1 us (15%)
  waiting for transfers between devices  5.01 us (6%)
  local copies, waits for them, and re-layouts  1.33 us (2%)
    all_to_all x1, blocking collectives, on_device(): parts = lax.all_to_all(partial, ('x', 'y'), 0, 0, tiled=True)  15.9 us
    all_to_all x1, starting transfers between devices, on_device(): lax.all_to_all(outgoing.reshape(NODES, 8, PAGEW), 'node', 0, 0, tiled=True)  15.8 us
    all_to_all x1, blocking collectives, on_device(): lax.all_to_all(block, ('x', 'y'), 0, 0, tiled=True).reshape(HALF, BLOCK)  15.1 us
    ppermute x1, starting transfers between devices, on_device(): other = lax.ppermute(gathered, 'core', swap)  9.08 us
    pallas_call x1, Pallas kernels, on_device(): pl.pallas_call(attend_kernel, out_shape=jax.ShapeDtypeStruct((SUFLEN, 2 *...  5.46 us
    ppermute x2, starting transfers between devices, on_device(): swapped = [lax.ppermute(part, 'core', swap) for part in send]  4.75 us
    pallas_call x1, Pallas kernels, on_device(): pl.pallas_call(down_kernel, out_shape=[jax.ShapeDtypeStruct((HALF, DOWN),...  3.38 us
    ppermute x1, waiting for transfers between devices, on_device(): other = lax.ppermute(gathered, 'core', swap)  2.41 us
  transfers between devices with their start and end apart: 4, of which 3 were waited for; matrix products, arithmetic and copies ran while one was open for 0% of the time, Pallas kernels for 4%

profile of v1, /device:TPU:1, one launch (start us, length us, event | category | flops | bytes accessed | tf_op | source)
XLA Modules:
  0.0 79.3 jit_solution(461513996285710362)
XLA Ops:
  0.0 2.0 %pages.1 = bf16[128,640]{1,0:T(8,128)(2,1)} custom-call(s32[1,16]{1,0:T(1,128)} %bitcast.14, s32[16,1,16]{2,1,0:T(1,128)} %bitcast.12, s32[16,16]{1,0:T(8,128)} %number_hbm.1, bf16[64,2,576]{2,1,0:T(2,128)(2,1)} %cache_hbm.1), custom_call_target="tpu_custom_call" | custom-call | flops 20000000 | bytes 300000 | tf_op jit(solution)/shard_map/pages/pallas_call | solution.py:300
  2.1 15.8 %all-to-all-start.1 = ((bf16[16,8,640]{2,1,0:T(8,128)(2,1)}), bf16[16,8,640]{2,1,0:T(8,128)(2,1)S(1)}, u32[]{:S(2)}, u32[]{:S(2)}) async-start(bf16[16,8,640]{2,1,0:T(8,128)(2,1)} %bitcast.16), calls=%async_computation.1 | async-start | bytes 327680 | tf_op jit(solution)/shard_map/all_to_all | solution.py:316
  17.8 3.4 %down.1 = (f32[128,2176]{1,0:T(8,128)}, f32[128,1024]{1,0:T(8,128)}, f32[128,1152]{1,0:T(8,128)}) custom-call(s32[16]{0:T(128)} %node_ref.3, s32[16]{0:T(128)} %adapter_ref.1, bf16[224,256]{1,0:T(8,128)(2,1)} %bitcast.18, bf16[224,1536]{1,0:T(8,128)(2,1)} %wq_hbm.1, bf16[224,576]{1,0:T(8,128)(2,1)} %wkv_hbm.1, bf16[4,64,224]{2,1,0:T(8,128)(2,1)} %bitcast.17), custom_call_target="tpu_custom_call" | custom-call | flops 1000 | bytes 1000 | tf_op jit(solution)/shard_map/down/pallas_call | solution.py:318
  21.2 2.8 %collective-permute-start.1 = (f32[128,1152]{1,0:T(8,128)}, f32[128,1152]{1,0:T(8,128)S(1)}, u32[]{:S(2)}, u32[]{:S(2)}) collective-permute-start(f32[128,1152]{1,0:T(8,128)} %get-tuple-element.12), channel_id=1, source_target_pairs={{0,1},{1,0},{2,3},{3,2},{4,5},{5,4},{6,7},{7,6},{8,9},{9,8},{10,11... | collective-permute-start | bytes 1769480 | tf_op jit(solution)/shard_map/ppermute | solution.py:343
  24.0 1.9 %collective-permute-start = (f32[128,1024]{1,0:T(8,128)}, f32[128,1024]{1,0:T(8,128)S(1)}, u32[]{:S(2)}, u32[]{:S(2)}) collective-permute-start(f32[128,1024]{1,0:T(8,128)} %get-tuple-element.11), channel_id=1, source_target_pairs={{0,1},{1,0},{2,3},{3,2},{4,5},{5,4},{6,7},{7,6},{8,9},{9,8},{10,11... | collective-permute-start | bytes 1572872 | tf_op jit(solution)/shard_map/ppermute | solution.py:343
  26.0 2.1 %collective-permute-done.refs_0_ = f32[128,1024]{1,0:T(8,128)S(1)} collective-permute-done((f32[128,1024]{1,0:T(8,128)}, f32[128,1024]{1,0:T(8,128)S(1)}, u32[]{:S(2)}, u32[]{:S(2)}) %collective-permute-start) | collective-permute-done | bytes 524320 | tf_op jit(solution)/shard_map/ppermute | solution.py:343
  28.1 0.0 collective-permute-done.1.refs_1_
  28.1 0.0 copy-start.1
  28.1 1.2 %copy-done.1 = f32[128,2176]{1,0:T(8,128)S(1)} copy-done((f32[128,2176]{1,0:T(8,128)S(1)}, f32[128,2176]{1,0:T(8,128)}, u32[]{:S(2)}) %copy-start.1) | copy-done | bytes 1114136
  29.3 0.0 copy-start.8
  29.3 0.0 copy-start.9
  29.3 0.0 copy-start.10
  29.3 0.0 copy-start.11
  29.3 0.0 copy-start.12
  29.3 0.0 copy-start.13
  29.3 0.0 copy-start.14
  29.4 0.0 copy-start.15
  29.4 0.1 add.1
  29.5 0.0 copy-start.2
  29.5 0.0 copy-start.3
  29.5 0.0 copy-start.4
  29.5 0.0 copy-start.7
  29.5 0.5 all-to-all-done.1
  30.0 15.9 %all_to_all.15.parts_ref = bf16[16,8,2176]{2,1,0:T(8,128)(2,1)S(1)} all-to-all(bf16[16,8,2176]{2,1,0:T(8,128)(2,1)S(1)} %bitcast.10), channel_id=1, replica_groups=mesh['node'=16,'x'=4,'y'=4,'core'=2] {'x','y'}, dimensions={0} | all-to-all | bytes 1114112 | tf_op jit(solution)/shard_map/all_to_all | solution.py:353
  46.0 0.0 copy-done.8
  46.0 0.0 copy-done.9
  46.0 0.0 copy-done.10
  46.0 0.0 copy-done.11
  46.0 0.0 copy-done.12
  46.0 0.0 copy-done.13
  46.0 0.0 copy-done.14
  46.0 0.0 copy-done.15
  46.0 0.0 copy-done.2
  46.1 0.0 copy-done.3
  46.1 0.0 copy-done.4
  46.1 0.0 copy-done.7
  46.1 1.2 %finish.1 = bf16[16,8,4480]{2,1,0:T(8,128)(2,1)S(1)} custom-call(s32[16]{0:T(128)S(1)} %copy-done.11, s32[16]{0:T(128)S(1)} %copy-done.14, s32[16]{0:T(128)S(1)} %copy-done.15, s32[1,16]{1,0:T(1,128)S(1)} %bitcast.15, s32[16,1,16]{2,1,0:T(1,128)S(1)} %bitcast.13, bf16[16,8,2176]{2,1,0:T(8,128)(2,1)S(1)} %all_to_all.15.parts_ref, ...), custom_call_target="tpu_custom_call" | custom-call | tf_op jit(solution)/shard_map/finish/pallas_call | solution.py:355
  47.3 0.0 copy-start
  47.3 0.0 copy-start.5
  47.3 0.0 copy-start.6
  47.3 15.1 %all_to_all.16 = bf16[16,8,4480]{2,1,0:T(8,128)(2,1)S(1)} all-to-all(bf16[16,8,4480]{2,1,0:T(8,128)(2,1)S(1)} %finish.1), channel_id=1, replica_groups=mesh['node'=16,'x'=4,'y'=4,'core'=2] {'x','y'}, dimensions={0} | all-to-all | bytes 2293760 | tf_op jit(solution)/shard_map/all_to_all | solution.py:376
  62.4 9.1 %collective-permute-start.2 = (bf16[128,4480]{1,0:T(8,128)(2,1)S(1)}, bf16[128,4480]{1,0:T(8,128)(2,1)S(1)}, u32[]{:S(2)}, u32[]{:S(2)}) collective-permute-start(bf16[128,4480]{1,0:T(8,128)(2,1)S(1)} %bitcast.8), channel_id=1, source_target_pairs={{0,1},{1,0},{2,3},{3,2},{4,5},{5,4},{6,7},{7,6},{8,9},{9,8},{10,11... | collective-permute-start | bytes 3440648 | tf_op jit(solution)/shard_map/ppermute | solution.py:377
  71.4 2.4 %collective-permute-done.2.other_ref = bf16[128,4480]{1,0:T(8,128)(2,1)S(1)} collective-permute-done((bf16[128,4480]{1,0:T(8,128)(2,1)S(1)}, bf16[128,4480]{1,0:T(8,128)(2,1)S(1)}, u32[]{:S(2)}, u32[]{:S(2)}) %collective-permute-start.2) | collective-permute-done | bytes 1146912 | tf_op jit(solution)/shard_map/ppermute | solution.py:377
  73.9 0.0 copy-done
  73.9 0.0 copy-done.5
  73.9 0.0 copy-done.6
  73.9 5.5 %attend.1 = bf16[256,256]{1,0:T(8,128)(2,1)} custom-call(s32[16]{0:T(128)S(1)} %copy-done.11, s32[16]{0:T(128)S(1)} %copy-done.15, bf16[128,4480]{1,0:T(8,128)(2,1)S(1)} %bitcast.9, bf16[128,4480]{1,0:T(8,128)(2,1)S(1)} %collective-permute-done.2.other_ref, bf16[1536,384]{1,0:T(8,128)(2,1)S(1)} %copy-done, bf16[2,128,512]{2,1,0:T(8,128)(2,1)S(1)} %copy-done.5, ...), custom_call_target="tpu_custom_call" | custom-call | tf_op jit(solution)/shard_map/attend/pallas_call | solution.py:378
Async XLA Ops:
  2.1 28.0 %all-to-all-start.1 = ((bf16[16,8,640]{2,1,0:T(8,128)(2,1)}), bf16[16,8,640]{2,1,0:T(8,128)(2,1)S(1)}, u32[]{:S(2)}, u32[]{:S(2)}) async-start(bf16[16,8,640]{2,1,0:T(8,128)(2,1)} %bitcast.16), calls=%async_computation.1 | async-start | bytes 327680 | tf_op jit(solution)/shard_map/all_to_all | solution.py:316
  21.2 6.9 %collective-permute-start.1 = (f32[128,1152]{1,0:T(8,128)}, f32[128,1152]{1,0:T(8,128)S(1)}, u32[]{:S(2)}, u32[]{:S(2)}) collective-permute-start(f32[128,1152]{1,0:T(8,128)} %get-tuple-element.12), channel_id=1, source_target_pairs={{0,1},{1,0},{2,3},{3,2},{4,5},{5,4},{6,7},{7,6},{8,9},{9,8},{10,11... | collective-permute-start | bytes 1769480 | tf_op jit(solution)/shard_map/ppermute | solution.py:343
  24.0 4.0 %collective-permute-start = (f32[128,1024]{1,0:T(8,128)}, f32[128,1024]{1,0:T(8,128)S(1)}, u32[]{:S(2)}, u32[]{:S(2)}) collective-permute-start(f32[128,1024]{1,0:T(8,128)} %get-tuple-element.11), channel_id=1, source_target_pairs={{0,1},{1,0},{2,3},{3,2},{4,5},{5,4},{6,7},{7,6},{8,9},{9,8},{10,11... | collective-permute-start | bytes 1572872 | tf_op jit(solution)/shard_map/ppermute | solution.py:343
  28.1 1.2 %copy-start.1 = (f32[128,2176]{1,0:T(8,128)S(1)}, f32[128,2176]{1,0:T(8,128)}, u32[]{:S(2)}) copy-start(f32[128,2176]{1,0:T(8,128)} %get-tuple-element.10.keep_ref) | copy-start | bytes 3342340
  29.3 16.7 %copy-start.8 = (f32[17,128]{1,0:T(8,128)S(1)}, f32[17,128]{1,0:T(8,128)}, u32[]{:S(2)}) copy-start(f32[17,128]{1,0:T(8,128)} %constant.9.clone.sb_ref) | copy-start | bytes 26116
  29.3 16.7 %copy-start.9 = (f32[17,128]{1,0:T(8,128)S(1)}, f32[17,128]{1,0:T(8,128)}, u32[]{:S(2)}) copy-start(f32[17,128]{1,0:T(8,128)} %constant.8.clone.cb_ref) | copy-start | bytes 26116
  29.3 16.7 %copy-start.10 = (s32[16,16,1]{1,2,0:T(1,128)S(1)}, s32[16,16,1]{1,2,0:T(1,128)}, u32[]{:S(2)}) copy-start(s32[16,16,1]{1,2,0:T(1,128)} %param.23) | copy-start | bytes 3076
  29.3 16.7 %copy-start.11 = (s32[16]{0:T(128)S(1)}, s32[16]{0:T(128)}, u32[]{:S(2)}) copy-start(s32[16]{0:T(128)} %node_ref.3) | copy-start | bytes 196
  29.3 16.7 %copy-start.12 = (f32[1536]{0:T(1024)S(1)}, f32[1536]{0:T(1024)}, u32[]{:S(2)}) copy-start(f32[1536]{0:T(1024)} %gq_ref.1) | copy-start | bytes 18436
  29.3 16.7 %copy-start.13 = (f32[512]{0:T(512)S(1)}, f32[512]{0:T(512)}, u32[]{:S(2)}) copy-start(f32[512]{0:T(512)} %gkv_ref.1) | copy-start | bytes 6148
  29.3 16.7 %copy-start.14 = (s32[16]{0:T(128)S(1)}, s32[16]{0:T(128)}, u32[]{:S(2)}) copy-start(s32[16]{0:T(128)} %adapter_ref.1) | copy-start | bytes 196
  29.4 16.7 %copy-start.15 = (s32[16]{0:T(128)S(1)}, s32[16]{0:T(128)}, u32[]{:S(2)}) copy-start(s32[16]{0:T(128)} %length_ref.3) | copy-start | bytes 196
  29.5 16.6 %copy-start.2 = (f32[256,128]{1,0:T(8,128)S(1)}, f32[256,128]{1,0:T(8,128)}, u32[]{:S(2)}) copy-start(f32[256,128]{1,0:T(8,128)} %constant.11.clone.st_ref) | copy-start | bytes 393220
  29.5 16.6 %copy-start.3 = (f32[256,128]{1,0:T(8,128)S(1)}, f32[256,128]{1,0:T(8,128)}, u32[]{:S(2)}) copy-start(f32[256,128]{1,0:T(8,128)} %constant.10.clone.ct_ref) | copy-start | bytes 393220
  29.5 16.6 %copy-start.4 = (bf16[4,32,1536]{2,1,0:T(8,128)(2,1)S(1)}, bf16[4,32,1536]{2,1,0:T(8,128)(2,1)}, u32[]{:S(2)}) copy-start(bf16[4,32,1536]{2,1,0:T(8,128)(2,1)} %aq_ref.1) | copy-start | bytes 1179652
  29.5 16.6 %copy-start.7 = (bf16[4,32,576]{2,1,0:T(8,128)(2,1)S(1)}, bf16[4,32,576]{2,1,0:T(8,128)(2,1)}, u32[]{:S(2)}) copy-start(bf16[4,32,576]{2,1,0:T(8,128)(2,1)} %akv_ref.1) | copy-start | bytes 442372
  47.3 26.6 %copy-start = (bf16[1536,384]{1,0:T(8,128)(2,1)S(1)}, bf16[1536,384]{1,0:T(8,128)(2,1)}, u32[]{:S(2)}) copy-start(bf16[1536,384]{1,0:T(8,128)(2,1)} %wq_ref.1) | copy-start | bytes 3538948
  47.3 26.6 %copy-start.5 = (bf16[2,128,512]{2,1,0:T(8,128)(2,1)S(1)}, bf16[2,128,512]{2,1,0:T(8,128)(2,1)}, u32[]{:S(2)}) copy-start(bf16[2,128,512]{2,1,0:T(8,128)(2,1)} %wk_ref.1) | copy-start | bytes 786436
  47.3 26.6 %copy-start.6 = (bf16[2,512,128]{2,1,0:T(8,128)(2,1)S(1)}, bf16[2,512,128]{2,1,0:T(8,128)(2,1)}, u32[]{:S(2)}) copy-start(bf16[2,512,128]{2,1,0:T(8,128)(2,1)} %wv_ref.1) | copy-start | bytes 786436
  62.4 11.5 %collective-permute-start.2 = (bf16[128,4480]{1,0:T(8,128)(2,1)S(1)}, bf16[128,4480]{1,0:T(8,128)(2,1)S(1)}, u32[]{:S(2)}, u32[]{:S(2)}) collective-permute-start(bf16[128,4480]{1,0:T(8,128)(2,1)S(1)} %bitcast.8), channel_id=1, source_target_pairs={{0,1},{1,0},{2,3},{3,2},{4,5},{5,4},{6,7},{7,6},{8,9},{9,8},{10,11... | collective-permute-start | bytes 3440648 | tf_op jit(solution)/shard_map/ppermute | solution.py:377

commit v2 on v1

--- a/solution.py
+++ b/solution.py
@@ -6,7 +6,6 @@
 from jax import lax
 from jax.experimental import pallas as pl
 from jax.experimental.pallas import tpu as pltpu
-from jax.sharding import Mesh
 from jax.sharding import PartitionSpec as P
 
 F32 = jnp.float32
@@ -27,6 +26,10 @@
 DOWN = Q + KEY + 2 * RANK
 CHUNKS = 4
 PAGEW = 640
+ROOT = 12
+CORNER = (2, 2)
+PLANE = [[((CORNER[0] + k // 4) % 4 * 4 + (CORNER[1] + k % 4) % 4) * 2 + c for k in range(CHIPS)] for c in range(2)]
+RING = [(ROOT + i) % NODES for i in range(NODES)]
 GROUPS = 1 + CHUNKS
 ROPES = Q + GROUPS * LATENT
 BLOCK = ROPES + 3 * 128
@@ -39,7 +42,6 @@
 NT = (((1,), (1,)), ((), ()))
 VMEM = pl.BlockSpec(memory_space=pltpu.VMEM)
 HBM = pl.BlockSpec(memory_space=pltpu.HBM)
-SMEM = pl.BlockSpec(memory_space=pltpu.SMEM)
 
 
 def mm(a, b):
@@ -62,31 +64,35 @@
     return [t.astype(np.float32) for t in (np.cos(base), np.sin(base), np.cos(step), np.sin(step))]
 
 
-def my_suffix(node_ref):
-    me = lax.axis_index("node")
-    mine = jnp.int32(0)
-    for s in range(NODES):
-        mine = jnp.where(node_ref[s] == me, s, mine)
-    return me, mine
-
-
-def down_kernel(
-    node_hbm, adapter_hbm, x_hbm, wq_hbm, wkv_hbm, panels_hbm, keep_ref, *refs
-):
-    send_refs, (node_ref, adapter_ref, x_ref, wq_ref, wkv_ref, panels_ref, sems) = refs[: len(SENDS)], refs[len(SENDS) :]
-    sources = (x_hbm, wq_hbm, wkv_hbm, panels_hbm, node_hbm, adapter_hbm)
-    targets = (x_ref, wq_ref, wkv_ref, panels_ref, node_ref, adapter_ref)
+def mine_of(row_ref, node_row):
+    served = node_row[...] == lax.axis_index("node")
+    return jnp.sum(jnp.where(served, row_ref[...], 0), axis=1, keepdims=True)
+
+
+def load(sources, targets, sems):
     copies = [pltpu.make_async_copy(src, dst, sems.at[i]) for i, (src, dst) in enumerate(zip(sources, targets))]
     for copy in copies:
         copy.start()
-    for copy in copies:
+    return copies
+
+
+def down_kernel(node_hbm, adapter_hbm, x_hbm, wq_hbm, wkv_hbm, panels_hbm, keep_ref, *refs):
+    send_refs, scratch, sems = refs[: len(SENDS)], refs[len(SENDS) : -1], refs[-1]
+    node_row, adapter_row, x_ref, wq_ref, wkv_ref, panels_ref = scratch
+    copies = load((x_hbm, wq_hbm, wkv_hbm, panels_hbm, node_hbm, adapter_hbm), (x_ref, wq_ref, wkv_ref, panels_ref, node_row, adapter_row), sems)
+    core = lax.axis_index("tp") % 2
+    copies[0].wait()
+    x = x_ref[...].T
+    copies[1].wait()
+    parts = [mm(x, wq_ref[:, lo : min(hi, Q)]) if lo < Q else None for lo, hi in SENDS]
+    for copy in copies[2:]:
         copy.wait()
-    _, mine = my_suffix(node_ref)
-    core = lax.axis_index("core")
-    x = x_ref[...].T
-    cut = SENDS[0][1]
-    tail = [mm(x, wq_ref[:, cut:]), mm(x, wkv_ref[...]), mmt(x, panels_ref[adapter_ref[mine]])]
-    parts = [mm(x, wq_ref[:, :cut]), jnp.concatenate(tail, axis=1)]
+    adapter = mine_of(adapter_row, node_row)
+    panel = jnp.zeros(panels_ref.shape[1:], F32)
+    for i in range(panels_ref.shape[0]):
+        panel = jnp.where(adapter == i, panels_ref[i].astype(F32), panel)
+    tail = [mm(x, wkv_ref[...]), mmt(x, panel.astype(BF16))]
+    parts[-1] = jnp.concatenate([parts[-1]] * (SENDS[-1][0] < Q) + tail, axis=1)
 
     @pl.when(core == 0)
     def _():
@@ -102,19 +108,12 @@
 
 
 def pages_kernel(node_hbm, owner_hbm, number_hbm, cache_hbm, pages_ref, node_row, owner_ref, number_ref, cache_ref, sems):
-    copies = [
-        pltpu.make_async_copy(source, target, sems.at[i])
-        for i, (source, target) in enumerate(
-            [(cache_hbm, cache_ref), (node_hbm, node_row), (owner_hbm, owner_ref), (number_hbm, number_ref)]
-        )
-    ]
-    for copy in copies:
-        copy.start()
+    copies = load((cache_hbm, node_hbm, owner_hbm, number_hbm), (cache_ref, node_row, owner_ref, number_ref), sems)
     for copy in copies[1:]:
         copy.wait()
     me = lax.axis_index("node")
     count = NODES * 8
-    node_of = iota((count, NODES), 0) // 8
+    node_of = (iota((count, NODES), 0) // 8 + ROOT) % NODES
     within = iota((count, 1), 0) % 8
     slot = within // 2
     expand = (node_row[...] == node_of).astype(BF16)
@@ -139,8 +138,9 @@
 
 
 def angles(length, rows, cb_ref, sb_ref, ct_ref, st_ref):
-    cb = cb_ref[pl.ds(length, 1), :]
-    sb = sb_ref[pl.ds(length, 1), :]
+    at = iota(cb_ref.shape, 0) == length
+    cb = jnp.sum(jnp.where(at, cb_ref[...], 0.0), axis=0, keepdims=True)
+    sb = jnp.sum(jnp.where(at, sb_ref[...], 0.0), axis=0, keepdims=True)
     ct = ct_ref[rows, :]
     st = st_ref[rows, :]
     return cb * ct - sb * st, sb * ct + cb * st
@@ -156,10 +156,9 @@
 
 
 def finish_kernel(
-    node_ref,
-    adapter_ref,
-    length_ref,
     node_row,
+    adapter_row,
+    length_row,
     owner_ref,
     parts_ref,
     pages_ref,
@@ -173,18 +172,25 @@
     st_ref,
     out_ref,
 ):
-    me, mine = my_suffix(node_ref)
-    adapter = adapter_ref[mine]
-    length = length_ref[mine]
-    core = lax.axis_index("core")
-    chip = lax.axis_index("x") * 4 + lax.axis_index("y")
-    first = pl.multiple_of(core * HALF + chip * ROWS, ROWS)
+    me = lax.axis_index("node")
+    adapter = mine_of(adapter_row, node_row)
+    length = mine_of(length_row, node_row)
+    core = lax.axis_index("tp") % 2
+    chip = lax.axis_index("tp") // 2
+    place = (chip // 4 + 4 - CORNER[0]) % 4 * 4 + (chip + 4 - CORNER[1]) % 4
+    first = pl.multiple_of(core * HALF + place * ROWS, ROWS)
     down = parts_ref[0].astype(F32)
     for i in range(1, CHIPS):
         down = down + parts_ref[i].astype(F32)
-    low = down[:, Q + KEY :].astype(BF16)
-    q_raw = down[:, :Q] + mm(low[:, :RANK], aq_ref[adapter])
-    kv_raw = down[:, Q : Q + KEY] + mm(low[:, RANK:], akv_ref[adapter])
+    count = aq_ref.shape[0] * RANK
+    chosen = iota((ROWS, count), 1) // RANK == adapter
+
+    def raised(low, up_ref):
+        low = jnp.where(chosen, jnp.concatenate([low] * aq_ref.shape[0], axis=1), 0.0).astype(BF16)
+        return mm(low, up_ref[...].reshape(count, up_ref.shape[2]))
+
+    q_raw = down[:, :Q] + raised(down[:, Q + KEY : Q + KEY + RANK], aq_ref)
+    kv_raw = down[:, Q : Q + KEY] + raised(down[:, Q + KEY + RANK :], akv_ref)
     q_lat = q_raw * lax.rsqrt(jnp.mean(q_raw * q_raw, axis=1, keepdims=True) + 1e-06) * gq_ref[...][None, :]
     c = kv_raw[:, :LATENT]
     c = c * lax.rsqrt(jnp.mean(c * c, axis=1, keepdims=True) + 1e-06) * gkv_ref[...][None, :]
@@ -200,7 +206,7 @@
     holder = jnp.sum(jnp.where(lane == entry, mine_owner, 0.0), axis=1, keepdims=True)
     earlier = (mine_owner == holder) & (lane < entry)
     rank = jnp.sum(earlier.astype(F32), axis=1, keepdims=True)
-    source = holder.astype(jnp.int32) * 8 + rank.astype(jnp.int32) * 2 + iota((count, 1), 0) % 2
+    source = (holder.astype(jnp.int32) + (NODES - ROOT)) % NODES * 8 + rank.astype(jnp.int32) * 2 + iota((count, 1), 0) % 2
     select = (iota((count, 128), 1) == source).astype(BF16)
     prefix = mm(select, pages_ref[...])[:, :KEY]
     chunks = [prefix[g * ROWS : (g + 1) * ROWS] for g in range(CHUNKS)]
@@ -212,11 +218,10 @@
 
 
 def attend_kernel(
-    node_ref, length_ref, mine_ref, other_ref, wq_ref, wk_ref, wv_ref, cb_ref, sb_ref, ct_ref, st_ref, out_ref
+    node_row, length_row, mine_ref, other_ref, wq_ref, wk_ref, wv_ref, cb_ref, sb_ref, ct_ref, st_ref, out_ref
 ):
-    _, mine = my_suffix(node_ref)
-    length = length_ref[mine]
-    core = lax.axis_index("core")
+    length = mine_of(length_row, node_row)
+    core = lax.axis_index("tp") % 2
     rows_a = pl.ds(pl.multiple_of(core * HALF, HALF), HALF)
     rows_b = pl.ds(pl.multiple_of((1 - core) * HALF, HALF), HALF)
 
@@ -261,9 +266,8 @@
     for w in weights[1:]:
         total = total + w
     total = jnp.sum(total, axis=1, keepdims=True)
-    mixed = jnp.zeros((count, LATENT), F32)
-    for g in range(GROUPS):
-        mixed = mixed + mm(weights[g].astype(BF16), latents[g])
+    weights = jnp.concatenate([w.astype(BF16) for w in weights], axis=1)
+    mixed = mm(weights, jnp.concatenate(latents, axis=0))
     latent = (mixed / total).astype(BF16)
     for h in range(2):
         values = mm(latent[h * SUFLEN : (h + 1) * SUFLEN], wv_ref[h]).astype(BF16)
@@ -290,12 +294,15 @@
     key_up_weight,
     value_up_weight,
 ):
-    alone = pltpu.CompilerParams(vmem_limit_bytes=60 * 1024 * 1024)
     params = pltpu.CompilerParams(vmem_limit_bytes=40 * 1024 * 1024)
     tables = [jnp.asarray(t) for t in rope_tables()]
     owner = jnp.transpose(page_owner, (0, 2, 1))
-    node_row = suffix_node.reshape(1, NODES)
-    swap = [(0, 1), (1, 0)]
+    node_row, adapter_row, length_row = [a.reshape(1, NODES) for a in (suffix_node, suffix_adapter, prefix_page_count)]
+
+    def far(*arrays):
+        return [pltpu.with_memory_space_constraint(a, pltpu.HBM) for a in arrays]
+
+    swap = [(i, i ^ 1) for i in range(2 * CHIPS)]
 
     outgoing = pl.pallas_call(
         pages_kernel,
@@ -309,11 +316,11 @@
             pltpu.VMEM(prefix_cache.shape, BF16),
             pltpu.SemaphoreType.DMA((4,)),
         ],
-        compiler_params=alone,
+        compiler_params=params,
         cost_estimate=pl.CostEstimate(flops=20_000_000, bytes_accessed=300_000, transcendentals=0),
         name="pages",
-    )(node_row, owner, page_number, prefix_cache)
-    received = lax.all_to_all(outgoing.reshape(NODES, 8, PAGEW), "node", 0, 0, tiled=True)
+    )(*far(node_row, owner, page_number, prefix_cache))
+    received = lax.all_to_all(outgoing.reshape(NODES, 8, PAGEW), "node", 0, 0, tiled=True, axis_index_groups=[RING])
     hidden, _ = lax.optimization_barrier((suffix_hidden, outgoing))
     keep, *send = pl.pallas_call(
         down_kernel,
@@ -321,26 +328,19 @@
         in_specs=[HBM] * 6,
         out_specs=[VMEM] * (1 + len(SENDS)),
         scratch_shapes=[
-            pltpu.SMEM((NODES,), jnp.int32),
-            pltpu.SMEM((NODES,), jnp.int32),
+            pltpu.VMEM((1, NODES), jnp.int32),
+            pltpu.VMEM((1, NODES), jnp.int32),
             pltpu.VMEM((224, SUFLEN), BF16),
             pltpu.VMEM((224, Q), BF16),
             pltpu.VMEM((224, KEY), BF16),
             pltpu.VMEM((4, 2 * RANK, 224), BF16),
             pltpu.SemaphoreType.DMA((6,)),
         ],
-        compiler_params=alone,
+        compiler_params=params,
         cost_estimate=pl.CostEstimate(flops=1000, bytes_accessed=1000, transcendentals=0),
         name="down",
-    )(
-        suffix_node,
-        suffix_adapter,
-        hidden.T,
-        query_down_weight,
-        kv_down_weight,
-        jnp.transpose(adapter_down_panels, (0, 2, 1)),
-    )
-    swapped = [lax.ppermute(part, "core", swap) for part in send]
+    )(*far(node_row, adapter_row, hidden.T, query_down_weight, kv_down_weight, jnp.transpose(adapter_down_panels, (0, 2, 1))))
+    swapped = [lax.ppermute(part, "tp", swap) for part in send]
     partial = pl.pallas_call(
         add_kernel,
         out_shape=jax.ShapeDtypeStruct((HALF, DOWN), BF16),
@@ -350,20 +350,19 @@
         cost_estimate=pl.CostEstimate(flops=1000, bytes_accessed=1000, transcendentals=0),
         name="add",
     )(keep, *swapped).reshape(CHIPS, ROWS, DOWN)
-    parts = lax.all_to_all(partial, ("x", "y"), 0, 0, tiled=True)
+    parts = lax.all_to_all(partial, "tp", 0, 0, tiled=True, axis_index_groups=PLANE)
 
     block = pl.pallas_call(
         finish_kernel,
         out_shape=jax.ShapeDtypeStruct((CHIPS, ROWS, BLOCK), BF16),
-        in_specs=[SMEM] * 3 + [VMEM] * 12,
+        in_specs=[VMEM] * 14,
         out_specs=VMEM,
         compiler_params=params,
         name="finish",
     )(
-        suffix_node,
-        suffix_adapter,
-        prefix_page_count,
         node_row,
+        adapter_row,
+        length_row,
         owner,
         parts,
         received.reshape(NODES * 8, PAGEW),
@@ -373,18 +372,18 @@
         latent_kv_gain,
         *tables,
     )
-    gathered = lax.all_to_all(block, ("x", "y"), 0, 0, tiled=True).reshape(HALF, BLOCK)
-    other = lax.ppermute(gathered, "core", swap)
+    gathered = lax.all_to_all(block, "tp", 0, 0, tiled=True, axis_index_groups=PLANE).reshape(HALF, BLOCK)
+    other = lax.ppermute(gathered, "tp", swap)
     return pl.pallas_call(
         attend_kernel,
         out_shape=jax.ShapeDtypeStruct((SUFLEN, 2 * VDIM), BF16),
-        in_specs=[SMEM] * 2 + [VMEM] * 9,
+        in_specs=[VMEM] * 11,
         out_specs=VMEM,
         compiler_params=params,
         name="attend",
     )(
-        suffix_node,
-        prefix_page_count,
+        node_row,
+        length_row,
         gathered,
         other,
         query_up_weight,
@@ -395,30 +394,28 @@
 
 
 def solution(mesh):
-    inner = Mesh(mesh.devices.reshape(NODES, 4, 4, 2), ("node", "x", "y", "core"))
-    tp = ("x", "y", "core")
     return jax.shard_map(
         on_device,
-        mesh=inner,
+        mesh=mesh,
         in_specs=(
-            P("node", tp),
-            P(),
-            P(),
-            P(),
-            P(),
-            P(),
-            P("node", tp, None),
-            P(tp, None),
-            P(tp, None),
-            P(None, tp, None),
-            P(),
-            P(),
-            P(),
-            P(),
-            P(None, tp),
-            P(tp, None, None),
-            P(tp, None, None),
+            P("node", "tp"),
+            P(),
+            P(),
+            P(),
+            P(),
+            P(),
+            P("node", "tp", None),
+            P("tp", None),
+            P("tp", None),
+            P(None, "tp", None),
+            P(),
+            P(),
+            P(),
+            P(),
+            P(None, "tp"),
+            P("tp", None, None),
+            P("tp", None, None),
         ),
-        out_specs=P("node", tp),
+        out_specs=P("node", "tp"),
         check_vma=False,
     )

time: 80.1 us -> 73.8 us (0.921)
  Pallas kernels: 12.1 us -> 8.83 us
  blocking collectives: 31 us -> 29.1 us
  local copies, waits for them, and re-layouts: 1.33 us -> 0.08 us
  starting transfers between devices: 29.6 us -> 28.5 us
    all_to_all x2, blocking collectives: 31 us -> 29.1 us  [the longest x1 16.4 us: on_device(): lax.all_to_all(block, 'tp', 0, 0, tiled=True, axis_index_groups=PLANE)]
    pallas_call x1, Pallas kernels: 5.46 us -> 3.91 us  [on_device(): pl.pallas_call(attend_kernel, out_shape=jax.ShapeDtypeStruct((SUFLEN, 2 *...]
    pallas_call x1, Pallas kernels: 3.38 us -> 2.1 us  [on_device(): pl.pallas_call(down_kernel, out_shape=[jax.ShapeDtypeStruct((HALF, DOWN),...]
    ppermute x3, starting transfers between devices: 13.8 us -> 12.6 us  [the longest x1 7.53 us: on_device(): other = lax.ppermute(gathered, 'tp', swap)]
    unnamed x32 -> x30, local copies, waits for them, and re-layouts: 1.33 us -> 0.08 us
  transfers between devices with their start and end apart: 4 -> 4, of which waited for: 3 -> 3; matrix products, arithmetic and copies ran while one was open for 0% -> 0% of each run, Pallas kernels for 4% -> 3%
where the time goes in v2:
time: 73.8 us; the launch traced here: 72.3 us
  blocking collectives  29.1 us (39%)
  starting transfers between devices  28.5 us (39%)
  Pallas kernels  8.83 us (12%)
  waiting for transfers between devices  5.58 us (8%)
    all_to_all x1, blocking collectives, on_device(): lax.all_to_all(block, 'tp', 0, 0, tiled=True, axis_index_groups=PLANE)  16.4 us
    all_to_all x1, starting transfers between devices, on_device(): lax.all_to_all(outgoing.reshape(NODES, 8, PAGEW), 'node', 0, 0, tiled=Tru...  15.9 us
    all_to_all x1, blocking collectives, on_device(): lax.all_to_all(partial, 'tp', 0, 0, tiled=True, axis_index_groups=PLANE)  12.7 us
    ppermute x1, starting transfers between devices, on_device(): other = lax.ppermute(gathered, 'tp', swap)  7.53 us
    ppermute x2, starting transfers between devices, on_device(): swapped = [lax.ppermute(part, 'tp', swap) for part in send]  5.04 us
    pallas_call x1, Pallas kernels, on_device(): pl.pallas_call(attend_kernel, out_shape=jax.ShapeDtypeStruct((SUFLEN, 2 *...  3.91 us
    ppermute x1, waiting for transfers between devices, on_device(): other = lax.ppermute(gathered, 'tp', swap)  2.41 us
    pallas_call x1, Pallas kernels, on_device(): pl.pallas_call(down_kernel, out_shape=[jax.ShapeDtypeStruct((HALF, DOWN),...  2.1 us
  transfers between devices with their start and end apart: 4, of which 3 were waited for; matrix products, arithmetic and copies ran while one was open for 0% of the time, Pallas kernels for 3%

profile of v2, /device:TPU:1, one launch (start us, length us, event | category | flops | bytes accessed | tf_op | source)
XLA Modules:
  0.0 72.3 jit_solution(7990393205052970994)
XLA Ops:
  0.0 2.1 %pages.1 = bf16[128,640]{1,0:T(8,128)(2,1)} custom-call(s32[1,16]{1,0:T(1,128)} %bitcast.16, s32[16,1,16]{2,1,0:T(1,128)} %bitcast.14, s32[16,16]{1,0:T(8,128)} %number_hbm.1, bf16[64,2,576]{2,1,0:T(2,128)(2,1)} %cache_hbm.1), custom_call_target="tpu_custom_call" | custom-call | flops 20000000 | bytes 300000 | tf_op jit(solution)/shard_map/pages/pallas_call | solution.py:307
  2.1 15.9 %all-to-all-start.1 = ((bf16[16,8,640]{2,1,0:T(8,128)(2,1)}), bf16[16,8,640]{2,1,0:T(8,128)(2,1)S(1)}, u32[]{:S(2)}, u32[]{:S(2)}) async-start(bf16[16,8,640]{2,1,0:T(8,128)(2,1)} %bitcast.7), calls=%async_computation.1 | async-start | bytes 327680 | tf_op jit(solution)/shard_map/all_to_all | solution.py:323
  18.0 2.1 %down.1 = (f32[128,2176]{1,0:T(8,128)S(1)}, f32[128,1024]{1,0:T(8,128)S(1)}, f32[128,1152]{1,0:T(8,128)S(1)}) custom-call(s32[1,16]{1,0:T(1,128)} %bitcast.17, s32[1,16]{1,0:T(1,128)} %bitcast.20, bf16[224,256]{1,0:T(8,128)(2,1)} %bitcast.25, bf16[224,1536]{1,0:T(8,128)(2,1)} %wq_hbm.1, bf16[224,576]{1,0:T(8,128)(2,1)} %wkv_hbm.1, bf16[4,64,224]{2,1,0:T(8,128)(2,1)} %bitcast.24), custom_call_target="tpu_custom_call" | custom-call | flops 1000 | bytes 1000 | tf_op jit(solution)/shard_map/down/pallas_call | solution.py:325
  20.1 3.1 %collective-permute-start.1 = (f32[128,1152]{1,0:T(8,128)S(1)}, f32[128,1152]{1,0:T(8,128)S(1)}, u32[]{:S(2)}, u32[]{:S(2)}) collective-permute-start(f32[128,1152]{1,0:T(8,128)S(1)} %get-tuple-element.12), channel_id=1, source_target_pairs={{0,1},{1,0},{2,3},{3,2},{4,5},{5,4},{6,7},{7,6},{8,9},{9,8},{10,11... | collective-permute-start | bytes 1769480 | tf_op jit(solution)/shard_map/ppermute | solution.py:343
  23.3 1.9 %collective-permute-start = (f32[128,1024]{1,0:T(8,128)S(1)}, f32[128,1024]{1,0:T(8,128)S(1)}, u32[]{:S(2)}, u32[]{:S(2)}) collective-permute-start(f32[128,1024]{1,0:T(8,128)S(1)} %get-tuple-element.11), channel_id=1, source_target_pairs={{0,1},{1,0},{2,3},{3,2},{4,5},{5,4},{6,7},{7,6},{8,9},{9,8},{10,11... | collective-permute-start | bytes 1572872 | tf_op jit(solution)/shard_map/ppermute | solution.py:343
  25.2 1.9 %collective-permute-done.refs_0_ = f32[128,1024]{1,0:T(8,128)S(1)} collective-permute-done((f32[128,1024]{1,0:T(8,128)S(1)}, f32[128,1024]{1,0:T(8,128)S(1)}, u32[]{:S(2)}, u32[]{:S(2)}) %collective-permute-start) | collective-permute-done | bytes 524320 | tf_op jit(solution)/shard_map/ppermute | solution.py:343
  27.1 0.0 collective-permute-done.1.refs_1_
  27.1 0.0 copy-start.7
  27.1 0.0 copy-start.8
  27.1 0.0 copy-start.9
  27.1 0.0 copy-start.10
  27.1 0.0 copy-start.11
  27.1 0.0 copy-start.12
  27.1 0.0 copy-start.13
  27.1 0.0 copy-start.14
  27.1 0.1 add.1
  27.2 0.0 copy-start.1
  27.3 0.0 copy-start.2
  27.3 0.0 copy-start.3
  27.3 0.0 copy-start.6
  27.3 1.3 %all-to-all-done.1 = bf16[16,8,640]{2,1,0:T(8,128)(2,1)S(1)} async-done(((bf16[16,8,640]{2,1,0:T(8,128)(2,1)}), bf16[16,8,640]{2,1,0:T(8,128)(2,1)S(1)}, u32[]{:S(2)}, u32[]{:S(2)}) %all-to-all-start.1) | async-done | bytes 163872 | tf_op jit(solution)/shard_map/all_to_all | solution.py:323
  28.6 12.7 %all_to_all.15.parts_ref = bf16[16,8,2176]{2,1,0:T(8,128)(2,1)S(1)} all-to-all(bf16[16,8,2176]{2,1,0:T(8,128)(2,1)S(1)} %bitcast.12), channel_id=1, replica_groups={{20,22,16,18,28,30,24,26,4,6,0,2,12,14,8,10},{21,23,17,19,29,31,25,27,5..., dimensions={0} | all-to-all | bytes 1114112 | tf_op jit(solution)/shard_map/all_to_all | solution.py:353
  41.3 0.0 copy-done.7
  41.3 0.0 copy-done.8
  41.3 0.0 copy-done.9
  41.3 0.0 copy-done.10
  41.4 0.0 copy-done.11
  41.4 0.0 copy-done.12
  41.4 0.0 copy-done.13
  41.4 0.0 copy-done.14
  41.4 0.0 copy-done.1
  41.4 0.0 copy-done.2
  41.4 0.0 copy-done.3
  41.4 0.0 copy-done.6
  41.4 0.6 finish.1
  42.1 0.0 copy-start
  42.1 0.0 copy-start.4
  42.1 0.0 copy-start.5
  42.1 16.4 %all_to_all.16 = bf16[16,8,4480]{2,1,0:T(8,128)(2,1)S(1)} all-to-all(bf16[16,8,4480]{2,1,0:T(8,128)(2,1)S(1)} %finish.1), channel_id=1, replica_groups={{20,22,16,18,28,30,24,26,4,6,0,2,12,14,8,10},{21,23,17,19,29,31,25,27,5..., dimensions={0} | all-to-all | bytes 2293760 | tf_op jit(solution)/shard_map/all_to_all | solution.py:375
  58.5 7.5 %collective-permute-start.2 = (bf16[128,4480]{1,0:T(8,128)(2,1)S(1)}, bf16[128,4480]{1,0:T(8,128)(2,1)S(1)}, u32[]{:S(2)}, u32[]{:S(2)}) collective-permute-start(bf16[128,4480]{1,0:T(8,128)(2,1)S(1)} %bitcast.10), channel_id=1, source_target_pairs={{0,1},{1,0},{2,3},{3,2},{4,5},{5,4},{6,7},{7,6},{8,9},{9,8},{10,11... | collective-permute-start | bytes 3440648 | tf_op jit(solution)/shard_map/ppermute | solution.py:376
  66.0 2.4 %collective-permute-done.2.other_ref = bf16[128,4480]{1,0:T(8,128)(2,1)S(1)} collective-permute-done((bf16[128,4480]{1,0:T(8,128)(2,1)S(1)}, bf16[128,4480]{1,0:T(8,128)(2,1)S(1)}, u32[]{:S(2)}, u32[]{:S(2)}) %collective-permute-start.2) | collective-permute-done | bytes 1146912 | tf_op jit(solution)/shard_map/ppermute | solution.py:376
  68.4 0.0 copy-done
  68.4 0.0 copy-done.4
  68.4 0.0 copy-done.5
  68.4 3.9 %attend.1 = bf16[256,256]{1,0:T(8,128)(2,1)} custom-call(s32[1,16]{1,0:T(1,128)S(1)} %bitcast.19, s32[1,16]{1,0:T(1,128)S(1)} %bitcast.23, bf16[128,4480]{1,0:T(8,128)(2,1)S(1)} %bitcast.11, bf16[128,4480]{1,0:T(8,128)(2,1)S(1)} %collective-permute-done.2.other_ref, bf16[1536,384]{1,0:T(8,128)(2,1)S(1)} %copy-done, bf16[2,128,512]{2,1,0:T(8,128)(2,1)S(1)} %copy-done.4, ...), custom_call_target="tpu_custom_call" | custom-call | tf_op jit(solution)/shard_map/attend/pallas_call | solution.py:377
Async XLA Ops:
  2.1 26.5 %all-to-all-start.1 = ((bf16[16,8,640]{2,1,0:T(8,128)(2,1)}), bf16[16,8,640]{2,1,0:T(8,128)(2,1)S(1)}, u32[]{:S(2)}, u32[]{:S(2)}) async-start(bf16[16,8,640]{2,1,0:T(8,128)(2,1)} %bitcast.7), calls=%async_computation.1 | async-start | bytes 327680 | tf_op jit(solution)/shard_map/all_to_all | solution.py:323
  20.1 6.9 %collective-permute-start.1 = (f32[128,1152]{1,0:T(8,128)S(1)}, f32[128,1152]{1,0:T(8,128)S(1)}, u32[]{:S(2)}, u32[]{:S(2)}) collective-permute-start(f32[128,1152]{1,0:T(8,128)S(1)} %get-tuple-element.12), channel_id=1, source_target_pairs={{0,1},{1,0},{2,3},{3,2},{4,5},{5,4},{6,7},{7,6},{8,9},{9,8},{10,11... | collective-permute-start | bytes 1769480 | tf_op jit(solution)/shard_map/ppermute | solution.py:343
  23.3 3.8 %collective-permute-start = (f32[128,1024]{1,0:T(8,128)S(1)}, f32[128,1024]{1,0:T(8,128)S(1)}, u32[]{:S(2)}, u32[]{:S(2)}) collective-permute-start(f32[128,1024]{1,0:T(8,128)S(1)} %get-tuple-element.11), channel_id=1, source_target_pairs={{0,1},{1,0},{2,3},{3,2},{4,5},{5,4},{6,7},{7,6},{8,9},{9,8},{10,11... | collective-permute-start | bytes 1572872 | tf_op jit(solution)/shard_map/ppermute | solution.py:343
  27.1 14.3 %copy-start.7 = (f32[17,128]{1,0:T(8,128)S(1)}, f32[17,128]{1,0:T(8,128)}, u32[]{:S(2)}) copy-start(f32[17,128]{1,0:T(8,128)} %constant.9.clone.sb_ref) | copy-start | bytes 26116
  27.1 14.3 %copy-start.8 = (f32[17,128]{1,0:T(8,128)S(1)}, f32[17,128]{1,0:T(8,128)}, u32[]{:S(2)}) copy-start(f32[17,128]{1,0:T(8,128)} %constant.8.clone.cb_ref) | copy-start | bytes 26116
  27.1 14.3 %copy-start.9 = (s32[16,16,1]{1,2,0:T(1,128)S(1)}, s32[16,16,1]{1,2,0:T(1,128)}, u32[]{:S(2)}) copy-start(s32[16,16,1]{1,2,0:T(1,128)} %param.23) | copy-start | bytes 3076
  27.1 14.3 %copy-start.10 = (f32[1536]{0:T(1024)S(1)}, f32[1536]{0:T(1024)}, u32[]{:S(2)}) copy-start(f32[1536]{0:T(1024)} %gq_ref.1) | copy-start | bytes 18436
  27.1 14.3 %copy-start.11 = (s32[16]{0:T(128)S(1)}, s32[16]{0:T(128)}, u32[]{:S(2)}) copy-start(s32[16]{0:T(128)} %param.26) | copy-start | bytes 196
  27.1 14.3 %copy-start.12 = (f32[512]{0:T(512)S(1)}, f32[512]{0:T(512)}, u32[]{:S(2)}) copy-start(f32[512]{0:T(512)} %gkv_ref.1) | copy-start | bytes 6148
  27.1 14.3 %copy-start.13 = (s32[16]{0:T(128)S(1)}, s32[16]{0:T(128)}, u32[]{:S(2)}) copy-start(s32[16]{0:T(128)} %param.22) | copy-start | bytes 196
  27.1 14.3 %copy-start.14 = (s32[16]{0:T(128)S(1)}, s32[16]{0:T(128)}, u32[]{:S(2)}) copy-start(s32[16]{0:T(128)} %param.25) | copy-start | bytes 196
  27.2 14.1 %copy-start.1 = (f32[256,128]{1,0:T(8,128)S(1)}, f32[256,128]{1,0:T(8,128)}, u32[]{:S(2)}) copy-start(f32[256,128]{1,0:T(8,128)} %constant.11.clone.st_ref) | copy-start | bytes 393220
  27.3 14.1 %copy-start.2 = (f32[256,128]{1,0:T(8,128)S(1)}, f32[256,128]{1,0:T(8,128)}, u32[]{:S(2)}) copy-start(f32[256,128]{1,0:T(8,128)} %constant.10.clone.ct_ref) | copy-start | bytes 393220
  27.3 14.1 %copy-start.3 = (bf16[4,32,1536]{2,1,0:T(8,128)(2,1)S(1)}, bf16[4,32,1536]{2,1,0:T(8,128)(2,1)}, u32[]{:S(2)}) copy-start(bf16[4,32,1536]{2,1,0:T(8,128)(2,1)} %aq_ref.1) | copy-start | bytes 1179652
  27.3 14.1 %copy-start.6 = (bf16[4,32,576]{2,1,0:T(8,128)(2,1)S(1)}, bf16[4,32,576]{2,1,0:T(8,128)(2,1)}, u32[]{:S(2)}) copy-start(bf16[4,32,576]{2,1,0:T(8,128)(2,1)} %akv_ref.1) | copy-start | bytes 442372
  42.1 26.3 %copy-start = (bf16[1536,384]{1,0:T(8,128)(2,1)S(1)}, bf16[1536,384]{1,0:T(8,128)(2,1)}, u32[]{:S(2)}) copy-start(bf16[1536,384]{1,0:T(8,128)(2,1)} %wq_ref.1) | copy-start | bytes 3538948
  42.1 26.3 %copy-start.4 = (bf16[2,128,512]{2,1,0:T(8,128)(2,1)S(1)}, bf16[2,128,512]{2,1,0:T(8,128)(2,1)}, u32[]{:S(2)}) copy-start(bf16[2,128,512]{2,1,0:T(8,128)(2,1)} %wk_ref.1) | copy-start | bytes 786436
  42.1 26.3 %copy-start.5 = (bf16[2,512,128]{2,1,0:T(8,128)(2,1)S(1)}, bf16[2,512,128]{2,1,0:T(8,128)(2,1)}, u32[]{:S(2)}) copy-start(bf16[2,512,128]{2,1,0:T(8,128)(2,1)} %wv_ref.1) | copy-start | bytes 786436
  58.5 9.9 %collective-permute-start.2 = (bf16[128,4480]{1,0:T(8,128)(2,1)S(1)}, bf16[128,4480]{1,0:T(8,128)(2,1)S(1)}, u32[]{:S(2)}, u32[]{:S(2)}) collective-permute-start(bf16[128,4480]{1,0:T(8,128)(2,1)S(1)} %bitcast.10), channel_id=1, source_target_pairs={{0,1},{1,0},{2,3},{3,2},{4,5},{5,4},{6,7},{7,6},{8,9},{9,8},{10,11... | collective-permute-start | bytes 3440648 | tf_op jit(solution)/shard_map/ppermute | solution.py:376
